TPU v7x, 32 devices: a whole 2x2x4 slice. The times are simulated.
32 devices in a mesh: dp: 8 (over z, y), mp: 4 (over x, core).
Axes of the slice: x: 2, y: 2, z: 4, core: 2. Of those that a mesh axis runs over, the one named last changes fastest.
Arguments:
- current: bfloat16 [5120, 768], P('dp', 'mp'), may hold values from -6 to 6
- history: bfloat16 [12, 5120, 768], P(None, 'dp', 'mp'), may hold values from -6 to 6
- cotangent: bfloat16 [5120, 768], P('dp', 'mp'), may hold values from -15.3 to 15.3
- seq_lengths: int32 [8, 4], P('dp'), may hold values from 1 to 512, 640 in all within a row
- w_qkv: bfloat16 [2, 768, 2304], P(None, None, 'mp'), may hold values from -0.21875 to 0.21875
- w_out: bfloat16 [2, 768, 768], P(None, 'mp'), may hold values from -0.875 to 0.875
- w_up: bfloat16 [2, 768, 3072], P(None, None, 'mp'), may hold values from -0.21875 to 0.21875
- w_down: bfloat16 [2, 3072, 768], P(None, 'mp'), may hold values from -0.109375 to 0.109375
- gain_attn: float32 [2, 768], replicated, may hold values from 0.5 to 1.5
- gain_mlp: float32 [2, 768], replicated, may hold values from 0.5 to 1.5
- dwa_first: float32 [13], replicated, may hold values from 0.1 to 0.6
- dwa_second: float32 [14], replicated, may hold values from 0.1 to 0.6
Outputs:
- mixed: bfloat16 [5120, 768], P('dp', 'mp')
- grad_current: bfloat16 [5120, 768], P('dp', 'mp')
- grad_history: bfloat16 [12, 5120, 768], P(None, 'dp', 'mp')
- grad_qkv: float32 [2, 768, 2304], P(None, 'dp', 'mp')
- grad_out: float32 [2, 768, 768], P(None, 'mp', 'dp')
- grad_up: float32 [2, 768, 3072], P(None, 'dp', 'mp')
- grad_down: float32 [2, 3072, 768], P(None, 'mp', 'dp')
- grad_gain_attn: float32 [2, 768], replicated
- grad_gain_mlp: float32 [2, 768], replicated
- grad_dwa_first: float32 [13], replicated
- grad_dwa_second: float32 [14], replicated
Inputs may be any that keep to these rules, and one draw needn't show every extreme that they name: `seq_lengths`: each row sums to 640, and its largest entry is 512.
All inputs are finite; a program needn't handle non-finite values.
Results may differ from a plain program's by a relative error of at most 0.025.
Values may be sent and summed in bfloat16 or wider, within the bound.
A program may use at most 192 MiB of HBM per device.

v0:
```python
import jax
import jax.numpy as jnp
from jax import lax
from jax.sharding import PartitionSpec as P

HEAD_DIM = 64


epsilon = 1e-05


def normalize(values, gain):
    center = values - jnp.mean(values, -1, keepdims=True)
    spread = jnp.mean(center * center, -1, keepdims=True)
    return center * lax.rsqrt(spread + epsilon) * gain


def smooth(values):
    return jax.nn.gelu(values, approximate=True)


def tables(lengths, rows, head_dim):
    ends = jnp.cumsum(lengths)
    places = jnp.arange(rows, dtype=jnp.int32)
    passed = (places[:, None] >= ends[None, :]).astype(jnp.int32)
    segment = jnp.sum(passed, 1)
    starts = jnp.sum(passed * lengths[None, :], 1)
    offset = (places - starts).astype(jnp.float32)
    visible = (segment[:, None] == segment[None, :]) & (places[None, :] <= places[:, None])
    freqs = 10000.0 ** (-2.0 * jnp.arange(head_dim // 2, dtype=jnp.float32) / head_dim)
    angles = offset[:, None] * freqs[None, :]
    return (visible, jnp.cos(angles), jnp.sin(angles))


def rotate(values, cosine, sine):
    half = values.shape[-1] // 2
    first, second = (values[..., :half], values[..., half:])
    cosine, sine = (cosine[:, None, :], sine[:, None, :])
    return jnp.concatenate([first * cosine - second * sine, second * cosine + first * sine], -1)


def unrotate(grads, cosine, sine):
    half = grads.shape[-1] // 2
    first, second = (grads[..., :half], grads[..., half:])
    cosine, sine = (cosine[:, None, :], sine[:, None, :])
    return jnp.concatenate([first * cosine + second * sine, second * cosine - first * sine], -1)


def attend(queries, keys, values, visible, block_rows):
    rows, heads, width = queries.shape
    count = rows // block_rows
    scale = width ** (-0.5)

    def one_block(item):
        query_block, seen = item
        scores = (
            jnp.einsum("qhd,khd->hqk", query_block, keys, preferred_element_type=jnp.float32)
            * scale
        )
        scores = jnp.where(seen[None], scores, -1e30)
        top = jnp.max(scores, -1, keepdims=True)
        total = jnp.sum(jnp.exp(scores - top), -1, keepdims=True)
        logsum = top + jnp.log(total)
        probs = jnp.exp(scores - logsum).astype(jnp.bfloat16)
        result = jnp.einsum("hqk,khd->qhd", probs, values, preferred_element_type=jnp.float32)
        return (result, logsum[..., 0])

    results, logsums = lax.map(
        one_block,
        (
            queries.reshape(count, block_rows, heads, width),
            visible.reshape(count, block_rows, rows),
        ),
    )
    return (results.reshape(rows, heads, width), logsums)


def attend_back(queries, keys, values, grad_heads, logsums, visible, block_rows):
    rows, heads, width = queries.shape
    count = rows // block_rows
    scale = width ** (-0.5)

    def one_block(carry, item):
        key_total, value_total = carry
        query_block, grad_block, logsum, seen = item
        scores = (
            jnp.einsum("qhd,khd->hqk", query_block, keys, preferred_element_type=jnp.float32)
            * scale
        )
        scores = jnp.where(seen[None], scores, -1e30)
        probs = jnp.exp(scores - logsum[..., None])
        probs_low = probs.astype(jnp.bfloat16)
        results = jnp.einsum("hqk,khd->qhd", probs_low, values, preferred_element_type=jnp.float32)
        grad_probs = jnp.einsum(
            "qhd,khd->hqk", grad_block, values, preferred_element_type=jnp.float32
        )
        grad_scores = (
            probs * (grad_probs - jnp.sum(probs * grad_probs, -1, keepdims=True))
        ).astype(jnp.bfloat16)
        grad_query = (
            jnp.einsum("hqk,khd->qhd", grad_scores, keys, preferred_element_type=jnp.float32)
            * scale
        )
        key_total = (
            key_total
            + jnp.einsum(
                "hqk,qhd->khd", grad_scores, query_block, preferred_element_type=jnp.float32
            )
            * scale
        )
        value_total = value_total + jnp.einsum(
            "hqk,qhd->khd", probs_low, grad_block, preferred_element_type=jnp.float32
        )
        return ((key_total, value_total), (grad_query, results))

    zeros = jnp.zeros(keys.shape, jnp.float32)
    items = (
        queries.reshape(count, block_rows, heads, width),
        grad_heads.reshape(count, block_rows, heads, width),
        logsums,
        visible.reshape(count, block_rows, rows),
    )
    (grad_keys, grad_values), (grad_queries, results) = lax.scan(one_block, (zeros, zeros), items)
    return (
        grad_queries.reshape(rows, heads, width),
        grad_keys,
        grad_values,
        results.reshape(rows, heads, width),
    )


def project_heads(whole, w_q, gain_a, cosine, sine, heads):
    rows = whole.shape[0]
    inputs = whole.astype(jnp.float32)
    normed = normalize(inputs, gain_a).astype(jnp.bfloat16)
    projected = jnp.dot(normed, w_q, preferred_element_type=jnp.float32).reshape(
        rows, heads, 3, HEAD_DIM
    )
    queries = rotate(projected[:, :, 0], cosine, sine).astype(jnp.bfloat16)
    keys = rotate(projected[:, :, 1], cosine, sine).astype(jnp.bfloat16)
    values = projected[:, :, 2].astype(jnp.bfloat16)
    return (inputs, normed, queries, keys, values)


def forward_layer(slice_low, w_q, w_o, w_u, w_d, gain_a, gain_m, visible, cosine, sine, block_rows):
    heads = w_o.shape[0] // HEAD_DIM
    rows, width = slice_low.shape
    offset = lax.axis_index("mp") * width
    whole = lax.all_gather(slice_low, "mp", axis=1, tiled=True)
    inputs, normed, queries, keys, values = project_heads(whole, w_q, gain_a, cosine, sine, heads)
    attended, logsums = attend(queries, keys, values, visible, block_rows)
    attended_low = attended.reshape(rows, heads * HEAD_DIM).astype(jnp.bfloat16)
    partial_attn = jnp.dot(attended_low, w_o, preferred_element_type=jnp.float32)
    branch = lax.psum(partial_attn.astype(jnp.bfloat16), "mp").astype(jnp.float32)
    middle = inputs + branch
    normed_mid = normalize(middle, gain_m).astype(jnp.bfloat16)
    own_rows = lax.dynamic_slice_in_dim(middle, offset, width, 1)
    hidden = smooth(jnp.dot(normed_mid, w_u, preferred_element_type=jnp.float32)).astype(
        jnp.bfloat16
    )
    feed = lax.psum_scatter(
        jnp.dot(hidden, w_d, preferred_element_type=jnp.float32).astype(jnp.bfloat16),
        "mp",
        scatter_dimension=1,
        tiled=True,
    ).astype(jnp.float32)
    result = own_rows + feed
    return (result, (whole, middle, normed_mid, logsums))


def backward_layer(
    grad_slice,
    slice_low,
    saved,
    w_q,
    w_o,
    w_u,
    w_d,
    gain_a,
    gain_m,
    visible,
    cosine,
    sine,
    block_rows,
):
    whole_kept, norm_state, normed_mid, logsums = saved
    heads = w_o.shape[0] // HEAD_DIM
    rows, width = grad_slice.shape
    offset = lax.axis_index("mp") * width
    grad_low = grad_slice.astype(jnp.bfloat16)
    grad_whole = lax.all_gather(grad_low, "mp", axis=1, tiled=True)
    inputs, normed, queries, keys, values = project_heads(
        whole_kept, w_q, gain_a, cosine, sine, heads
    )
    pre_act = jnp.dot(normed_mid, w_u, preferred_element_type=jnp.float32)
    activation, smooth_pull = jax.vjp(smooth, pre_act)
    hidden = activation.astype(jnp.bfloat16)
    grad_down = jnp.einsum("tf,td->fd", hidden, grad_whole, preferred_element_type=jnp.float32)
    grad_hidden = jnp.einsum("td,fd->tf", grad_whole, w_d, preferred_element_type=jnp.float32)
    grad_pre = smooth_pull(grad_hidden)[0].astype(jnp.bfloat16)
    grad_up = jnp.einsum("td,tf->df", normed_mid, grad_pre, preferred_element_type=jnp.float32)
    grad_normed_mid = jnp.einsum("tf,df->td", grad_pre, w_u, preferred_element_type=jnp.float32)
    _, norm_pull = jax.vjp(normalize, norm_state, gain_m)
    part_mid, gain_mid = norm_pull(grad_normed_mid)
    grad_middle = grad_whole.astype(jnp.float32) + lax.psum(
        part_mid.astype(jnp.bfloat16), "mp"
    ).astype(jnp.float32)
    grad_branch = grad_middle.astype(jnp.bfloat16)
    own_middle = lax.dynamic_slice_in_dim(grad_middle, offset, width, 1)
    grad_heads = jnp.einsum("td,cd->tc", grad_branch, w_o, preferred_element_type=jnp.float32)
    grad_heads = grad_heads.astype(jnp.bfloat16).reshape(rows, heads, HEAD_DIM)
    grad_queries, grad_keys, grad_values, results = attend_back(
        queries, keys, values, grad_heads, logsums, visible, block_rows
    )
    results_low = results.reshape(rows, heads * HEAD_DIM).astype(jnp.bfloat16)
    grad_outw = jnp.einsum(
        "tc,td->cd", results_low, grad_branch, preferred_element_type=jnp.float32
    )
    grad_rows = jnp.stack(
        [unrotate(grad_queries, cosine, sine), unrotate(grad_keys, cosine, sine), grad_values], 2
    )
    grad_rows = grad_rows.astype(jnp.bfloat16).reshape(rows, heads * 3 * HEAD_DIM)
    grad_inw = jnp.einsum("td,tc->dc", normed, grad_rows, preferred_element_type=jnp.float32)
    grad_normed = jnp.einsum("tc,dc->td", grad_rows, w_q, preferred_element_type=jnp.float32)
    _, input_pull = jax.vjp(normalize, inputs, gain_a)
    part_in, gain_in = input_pull(grad_normed)
    grad_input = (
        lax.psum_scatter(
            part_in.astype(jnp.bfloat16), "mp", scatter_dimension=1, tiled=True
        ).astype(jnp.float32)
        + own_middle
    )
    return (grad_input, (grad_inw, grad_outw, grad_up, grad_down), gain_in, gain_mid)


def blend(coeffs, history):
    total = jnp.zeros(history.shape[1:], jnp.float32)
    for index in range(history.shape[0]):
        total = total + coeffs[index] * history[index].astype(jnp.float32)
    return total


def inner_terms(history, grads):
    return jnp.stack(
        [jnp.sum(history[index].astype(jnp.float32) * grads) for index in range(history.shape[0])]
    )


def shards(
    current,
    history,
    cotangent,
    seq_lengths,
    w_qkv,
    w_out,
    w_up,
    w_down,
    gain_attn,
    gain_mlp,
    dwa_first,
    dwa_second,
):
    rows = current.shape[0]
    past = history.shape[0]
    visible, cosine, sine = tables(seq_lengths[0], rows, HEAD_DIM)
    shared = (visible, cosine, sine, rows)

    def weights(layer):
        return (
            w_qkv[layer],
            w_out[layer],
            w_up[layer],
            w_down[layer],
            gain_attn[layer],
            gain_mlp[layer],
        )

    first_out, saved_first = forward_layer(current, *weights(0), *shared)
    following = (blend(dwa_first[:past], history) + dwa_first[past] * first_out).astype(
        jnp.bfloat16
    )
    second_out, saved_second = forward_layer(following, *weights(1), *shared)
    result = (
        blend(dwa_second[:past], history)
        + dwa_second[past] * first_out
        + dwa_second[past + 1] * second_out
    )
    mixed = result.astype(jnp.bfloat16)
    grad_mixed = cotangent.astype(jnp.float32)
    grad_next, grads_second, attn_second, mlp_second = backward_layer(
        dwa_second[past + 1] * grad_mixed, following, saved_second, *weights(1), *shared
    )
    grad_first_out = dwa_first[past] * grad_next + dwa_second[past] * grad_mixed
    grad_cur, grads_first, attn_first, mlp_first = backward_layer(
        grad_first_out, current, saved_first, *weights(0), *shared
    )
    together = tuple((jnp.stack([one, two]) for one, two in zip(grads_first, grads_second)))
    stacked = (
        lax.psum_scatter(together[0], "dp", scatter_dimension=1, tiled=True),
        lax.psum_scatter(together[1], "dp", scatter_dimension=2, tiled=True),
        lax.psum_scatter(together[2], "dp", scatter_dimension=1, tiled=True),
        lax.psum_scatter(together[3], "dp", scatter_dimension=2, tiled=True),
    )
    grad_hist = (
        dwa_first[:past, None, None] * grad_next[None]
        + dwa_second[:past, None, None] * grad_mixed[None]
    )
    hist_first = inner_terms(history, grad_next)
    hist_second = inner_terms(history, grad_mixed)
    part_first = jnp.concatenate([hist_first, jnp.sum(first_out * grad_next)[None]])
    part_second = jnp.concatenate(
        [hist_second, jnp.sum(first_out * grad_mixed)[None], jnp.sum(second_out * grad_mixed)[None]]
    )
    gains_attn = jnp.stack([attn_first, attn_second])
    gains_mlp = jnp.stack([mlp_first, mlp_second])
    total_first, total_second, total_attn, total_mlp = lax.psum(
        (part_first, part_second, gains_attn, gains_mlp), ("dp", "mp")
    )
    return (
        mixed,
        grad_cur.astype(jnp.bfloat16),
        grad_hist.astype(jnp.bfloat16),
        stacked[0],
        stacked[1],
        stacked[2],
        stacked[3],
        total_attn,
        total_mlp,
        total_first,
        total_second,
    )


def solution(mesh):
    in_specs = (
        P("dp", "mp"),
        P(None, "dp", "mp"),
        P("dp", "mp"),
        P("dp", None),
        P(None, None, "mp"),
        P(None, "mp", None),
        P(None, None, "mp"),
        P(None, "mp", None),
        P(),
        P(),
        P(),
        P(),
    )
    out_specs = (
        P("dp", "mp"),
        P("dp", "mp"),
        P(None, "dp", "mp"),
        P(None, "dp", "mp"),
        P(None, "mp", "dp"),
        P(None, "dp", "mp"),
        P(None, "mp", "dp"),
        P(),
        P(),
        P(),
        P(),
    )
    return jax.shard_map(shards, mesh=mesh, in_specs=in_specs, out_specs=out_specs, check_vma=False)
```

profile of v0, /device:TPU:0, one launch (start us, length us, event | category | flops | bytes accessed | tf_op | source)
XLA Modules:
  0.0 848.2 jit_solution(3406911438079140993)
XLA Ops:
  7.2 11.3 %all_gather.12 = bf16[640,768]{0,1:T(8,128)(2,1)S(1)} all-gather(bf16[640,192]{0,1:T(8,128)(2,1)} %param.12), channel_id=1, replica_groups=mesh['dp'=8,'mp'=4] {'mp'}, dimensions={1}, use_global_device_ids=true | all-gather | bytes 1228800 | tf_op jit(solution)/shard_map/all_gather | solution.py:149
  29.1 2.5 convolution_convert_fusion.7
  34.4 36.0 %all-reduce.10.cloned.1.call-done = bf16[640,768]{1,0:T(8,128)(2,1)} async-done(((bf16[640,768]{1,0:T(8,128)(2,1)}), bf16[640,768]{1,0:T(8,128)(2,1)}) %all-reduce.10.cloned.1.call-update) | async-done | bytes 983056 | tf_op jit(solution)/shard_map/psum | solution.py:154
  79.8 3.3 fusion.183
  106.8 12.1 %fusion.133 = bf16[640,192]{1,0:T(8,128)(2,1)} fusion(bf16[1,640,192]{2,1,0:T(8,128)(2,1)} %copy.208, bf16[1,640,192]{2,1,0:T(8,128)(2,1)} %copy.207, bf16[1,640,192]{2,1,0:T(8,128)(2,1)} %copy.206, bf16[1,640,192]{2,1,0:T(8,128)(2,1)} %copy.205, bf16[1,640,192]{2,1,0:T(8,128)(2,1)} %copy.204, bf16[1,640,192]{2,1,0:T(8,128)(2,1)} %copy.203, ...), kind=kLoop, calls=%fused_computation.256 | loop fusion | flops 4915200 | bytes 3932216 | tf_op jit(solution)/shard_map/convert_element_type | solution.py:279
  120.0 9.5 %all_gather.13 = bf16[640,768]{0,1:T(8,128)(2,1)} all-gather(bf16[640,192]{0,1:T(8,128)(2,1)S(1)} %copy.150), channel_id=1, replica_groups=mesh['dp'=8,'mp'=4] {'mp'}, dimensions={1}, use_global_device_ids=true | all-gather | bytes 1228800 | tf_op jit(solution)/shard_map/all_gather | solution.py:149
  144.8 16.9 %all_gather.14 = bf16[640,768]{0,1:T(8,128)(2,1)} all-gather(bf16[640,192]{0,1:T(8,128)(2,1)} %copy.157), channel_id=1, replica_groups=mesh['dp'=8,'mp'=4] {'mp'}, dimensions={1}, use_global_device_ids=true | all-gather | bytes 1228800 | tf_op jit(solution)/shard_map/all_gather | solution.py:191
  161.7 19.5 %all-reduce.12.cloned.1.call-done = bf16[640,768]{1,0:T(8,128)(2,1)} async-done(((bf16[640,768]{1,0:T(8,128)(2,1)}), bf16[640,768]{1,0:T(8,128)(2,1)}) %all-reduce.12.cloned.1.call-update) | async-done | bytes 983056 | tf_op jit(solution)/shard_map/psum | solution.py:154
  194.9 4.1 fusion.40
  199.3 29.3 %all-reduce.14.cloned.1.call-done = bf16[640,768]{1,0:T(8,128)(2,1)} async-done(((bf16[640,768]{1,0:T(8,128)(2,1)}), bf16[640,768]{1,0:T(8,128)(2,1)}) %all-reduce.14.cloned.1.call-update) | async-done | bytes 983056 | tf_op jit(solution)/shard_map/psum | solution.py:205
  230.7 4.4 multiply_reduce_fusion.1
  247.7 3.0 convert_add_fusion.3
  250.8 5.0 reduce-scatter.21.cloned.1.call-done
  257.6 25.3 %reduce-scatter.23.cloned.1.call-done = bf16[192,640]{1,0:T(8,128)(2,1)} async-done(((bf16[768,640]{1,0:T(8,128)(2,1)}), bf16[192,640]{1,0:T(8,128)(2,1)}) %reduce-scatter.23.cloned.1.call-update) | async-done | bytes 245776
  284.8 6.2 fusion.131
  295.9 9.9 %all_gather.15 = bf16[640,768]{0,1:T(8,128)(2,1)S(1)} all-gather(bf16[640,192]{0,1:T(8,128)(2,1)} %copy.163), channel_id=1, replica_groups=mesh['dp'=8,'mp'=4] {'mp'}, dimensions={1}, use_global_device_ids=true | all-gather | bytes 1228800 | tf_op jit(solution)/shard_map/all_gather | solution.py:191
  305.8 4.2 fusion.26
  316.4 33.8 %all-reduce.16.cloned.1.call-done = bf16[640,768]{1,0:T(8,128)(2,1)} async-done(((bf16[640,768]{1,0:T(8,128)(2,1)}), bf16[640,768]{1,0:T(8,128)(2,1)}) %all-reduce.16.cloned.1.call-update) | async-done | bytes 983056 | tf_op jit(solution)/shard_map/psum | solution.py:205
  352.3 4.4 multiply_reduce_fusion
  372.6 3.5 copy.195
  376.1 3.3 reshape.365
  379.7 3.5 convolution_bitcast_fusion
  389.7 8.2 copy.172
  402.2 7.5 copy.171
  410.4 2.9 convolution_bitcast_fusion.2
  414.7 2.5 pad_maximum_fusion
  420.5 12.8 %fusion.134 = bf16[640,192]{1,0:T(8,128)(2,1)} fusion(bf16[640,192]{1,0:T(8,128)(2,1)} %copy.190, f32[640,768]{1,0:T(8,128)} %get-tuple-element.231, s32[]{:T(128)S(6)} %select_n.20, bf16[1,640,192]{2,1,0:T(8,128)(2,1)} %copy.208, bf16[1,640,192]{2,1,0:T(8,128)(2,1)} %copy.207, bf16[1,640,192]{2,1,0:T(8,128)(2,1)} %copy.206, ...), kind=kLoop, calls=%fused_computation.257 | loop fusion | flops 5406720 | bytes 4669500 | tf_op jit(solution)/shard_map/convert_element_type | solution.py:288
  435.5 8.4 concatenate.46
  443.9 8.9 %concatenate.47 = f32[14]{0:T(128)S(1)} concatenate(f32[1]{0:T(128)} %bitcast.119, f32[1]{0:T(128)} %bitcast.120, f32[1]{0:T(128)} %bitcast.121, f32[1]{0:T(128)} %bitcast.122, f32[1]{0:T(128)} %bitcast.123, f32[1]{0:T(128)} %bitcast.124, f32[1]{0:T(128)} %bitcast.125, f32[1]{0:T(128)} %bitcast.126, f32[1]{0:T(128)} %bitcast.127, f32[1]{0:T(128)} %bitcast.128, f32[1]{0:T(128)} %bitcast.129, ...), dimensions={0} | concatenate | bytes 112 | tf_op jit(solution)/shard_map/concatenate | solution.py:311
  455.3 42.4 %all-reduce.2 = (f32[2,768]{1,0:T(2,128)}, f32[2,768]{1,0:T(2,128)}, f32[13]{0:T(128)}, f32[14]{0:T(128)}) all-reduce(f32[2,768]{1,0:T(2,128)S(1)} %pad_maximum_fusion.16, f32[2,768]{1,0:T(2,128)S(1)} %pad_maximum_fusion.17, f32[13]{0:T(128)S(1)} %concatenate.46, f32[14]{0:T(128)S(1)} %concatenate.47), channel_id=1, replica_groups=mesh['dp'=8,'mp'=4] {'dp','mp'}, use_global_device_ids=true, to_apply=%region_39.40 | all-reduce | flops 3099 | bytes 24792 | tf_op jit(solution)/shard_map/psum | solution.py:316
  504.6 237.9 %all-reduce.18.cloned.1.call-done = (f32[2,768,576]{2,0,1:T(2,128)}, f32[2,768,768]{1,0,2:T(2,128)}) async-done(((f32[2,768,576]{2,0,1:T(2,128)}, f32[2,768,768]{1,0,2:T(2,128)}), (f32[2,768,576]{2,0,1:T(2,128)}, f32[2,768,768]{1,0,2:T(2,128)})) %all-reduce.18.cloned.1.call-update) | async-done | bytes 8257552
  746.4 95.1 %reduce-scatter.17.cloned.1.call-done = f32[2,96,768]{2,1,0:T(8,128)} async-done(((f32[2,768,768]{2,1,0:T(8,128)}), f32[2,96,768]{2,1,0:T(8,128)}) %reduce-scatter.17.cloned.1.call-update) | async-done | bytes 589840 | tf_op jit(solution)/shard_map/reduce_scatter | solution.py:301
  (399 shorter events, 154.0 us)
Async XLA Ops:
  7.2 63.3 %all-reduce.10.cloned.1.call-start = ((), (), s32[]{:S(2)}) async-start(), calls=%async_computation.6 | async-start | bytes 1966080 | tf_op jit(solution)/shard_map/psum | solution.py:154
  20.7 111.6 %copy-start.85 = (f32[768]{0:T(1024)}, f32[768]{0:T(1024)S(1)}, u32[]{:S(2)}) copy-start(f32[768]{0:T(1024)S(1)} %get-tuple-element.198) | copy-start | bytes 9220
  33.7 71.1 %reduce-scatter.19.cloned.1.call-start = ((), (), s32[]{:S(2)}) async-start(), calls=%async_computation.11 | async-start | bytes 1228800
  34.4 39.4 %copy-start.78 = (f32[768]{0:T(1024)}, f32[768]{0:T(1024)S(1)}, u32[]{:S(2)}) copy-start(f32[768]{0:T(1024)S(1)} %get-tuple-element.200) | copy-start | bytes 9220
  79.3 101.9 %all-reduce.12.cloned.1.call-start = ((), (), s32[]{:S(2)}) async-start(), calls=%async_computation.7 | async-start | bytes 1966080 | tf_op jit(solution)/shard_map/psum | solution.py:154
  83.3 23.4 %copy-start.10 = (bf16[1,640,192]{2,1,0:T(8,128)(2,1)}, bf16[1,640,192]{2,1,0:T(8,128)(2,1)S(1)}, u32[]{:S(2)}) copy-start(bf16[1,640,192]{2,1,0:T(8,128)(2,1)S(1)} %copy.197) | copy-start | bytes 737284
  83.5 23.2 %copy-start.12 = (bf16[1,640,192]{2,1,0:T(8,128)(2,1)}, bf16[1,640,192]{2,1,0:T(8,128)(2,1)S(1)}, u32[]{:S(2)}) copy-start(bf16[1,640,192]{2,1,0:T(8,128)(2,1)S(1)} %copy.198) | copy-start | bytes 737284
  84.8 22.0 %copy-start.14 = (bf16[1,640,192]{2,1,0:T(8,128)(2,1)}, bf16[1,640,192]{2,1,0:T(8,128)(2,1)S(1)}, u32[]{:S(2)}) copy-start(bf16[1,640,192]{2,1,0:T(8,128)(2,1)S(1)} %copy.199) | copy-start | bytes 737284
  90.4 13.0 %copy-start.59 = (f32[13]{0:T(128)S(1)}, f32[13]{0:T(128)}, u32[]{:S(2)}) copy-start(f32[13]{0:T(128)} %param.22) | copy-start | bytes 160
  90.4 13.7 %copy-start.58 = (f32[14]{0:T(128)S(1)}, f32[14]{0:T(128)}, u32[]{:S(2)}) copy-start(f32[14]{0:T(128)} %param.23) | copy-start | bytes 172
  140.6 88.0 %all-reduce.14.cloned.1.call-start = ((), (), s32[]{:S(2)}) async-start(), calls=%async_computation.8 | async-start | bytes 1966080 | tf_op jit(solution)/shard_map/psum | solution.py:205
  182.9 6.4 copy-start.60
  183.4 5.9 copy-start.76
  192.6 63.2 %reduce-scatter.21.cloned.1.call-start = ((), (), s32[]{:S(2)}) async-start(), calls=%async_computation.12 | async-start | bytes 1228800
  199.1 83.9 %reduce-scatter.23.cloned.1.call-start = ((), (), s32[]{:S(2)}) async-start(), calls=%async_computation.13 | async-start | bytes 1228800
  230.6 4.4 slice-start.2
  230.7 4.4 slice-start.3
  247.7 102.6 %all-reduce.16.cloned.1.call-start = ((), (), s32[]{:S(2)}) async-start(), calls=%async_computation.9 | async-start | bytes 1966080 | tf_op jit(solution)/shard_map/psum | solution.py:205
  284.8 7.1 copy-start.6
  305.8 4.3 copy-start.81
  305.8 4.3 copy-start.103
  314.1 185.2 %reduce-scatter.25.cloned.1.call-start = ((), (), s32[]{:S(2)}) async-start(), calls=%async_computation.14 | async-start | bytes 1228800
  352.3 4.4 slice-start
  352.3 4.4 slice-start.1
  368.8 133.9 %reduce-scatter.27.cloned.1.call-start = ((), (), s32[]{:S(2)}) async-start(), calls=%async_computation.15 | async-start | bytes 1327104
  379.5 363.0 %all-reduce.18.cloned.1.call-start = ((), (), s32[]{:S(2)}) async-start(), calls=%async_computation.16 | async-start | bytes 17301504
  409.7 431.8 %reduce-scatter.17.cloned.1.call-start = ((), (), s32[]{:S(2)}) async-start(), calls=%async_computation.10 | async-start | bytes 5308416 | tf_op jit(solution)/shard_map/reduce_scatter | solution.py:301
  420.5 14.7 %copy-start.9 = (f32[640,192]{1,0:T(8,128)S(1)}, f32[640,192]{1,0:T(8,128)}, u32[]{:S(2)}) copy-start(f32[640,192]{1,0:T(8,128)} %copy-done.8) | copy-start | bytes 1474564
  420.5 15.0 %copy-start.97 = (f32[768]{0:T(1024)S(1)}, f32[768]{0:T(1024)}, u32[]{:S(2)}) copy-start(f32[768]{0:T(1024)} %get-tuple-element.163) | copy-start | bytes 9220
  433.4 19.4 %copy-start.26 = (f32[640,192]{0,1:T(8,128)S(1)}, f32[640,192]{0,1:T(8,128)}, u32[]{:S(2)}) copy-start(f32[640,192]{0,1:T(8,128)} %copy.170) | copy-start | bytes 1474564
  452.8 45.0 %copy-start.5 = (bf16[640,768]{1,0:T(8,128)(2,1)S(1)}, bf16[640,768]{1,0:T(8,128)(2,1)}, u32[]{:S(2)}) copy-start(bf16[640,768]{1,0:T(8,128)(2,1)} %copy.164) | copy-start | bytes 2949124
  452.8 44.9 %copy-start.25 = (bf16[640,768]{1,0:T(8,128)(2,1)S(1)}, bf16[640,768]{1,0:T(8,128)(2,1)}, u32[]{:S(2)}) copy-start(bf16[640,768]{1,0:T(8,128)(2,1)} %all-reduce.16.cloned.1.call-done) | copy-start | bytes 2949124
  (94 other events, 190.0 us)
Sparse Core Ops, SparseCore 0:
  33.9 36.5 all-reduce.9
  79.4 24.7 reduce-scatter.18
  140.7 40.4 all-reduce.11
  192.7 35.8 all-reduce.13
  231.0 24.7 reduce-scatter.20
  258.4 24.4 reduce-scatter.22
  314.2 35.9 all-reduce.15
  368.9 24.7 reduce-scatter.24
  397.1 64.2 reduce-scatter.26
  465.2 277.2 all-reduce.17
  747.2 94.2 reduce-scatter.16
where the time goes:
time: 858 us; the launch traced here: 848 us
  waiting for transfers between devices  482 us (56%)
  local copies, waits for them, and re-layouts  115 us (13%)
  blocking collectives  90.1 us (11%)
  other arithmetic  75.3 us (9%)
  matrix products  68.1 us (8%)
  between operations  16.4 us (2%)
    unnamed x17, waiting for transfers between devices  268 us
    reduce_scatter x1, waiting for transfers between devices, shards(): lax.psum_scatter(together[2], 'dp', scatter_dimension=1, tiled=True)  95.1 us
    psum x2, waiting for transfers between devices, backward_layer(): lax.psum(part_mid.astype(jnp.bfloat16), 'mp').astype(jnp.float32)  63.1 us
    unnamed x260, local copies, waits for them, and re-layouts  62.6 us
    psum x2, waiting for transfers between devices, forward_layer(): lax.psum(partial_attn.astype(jnp.bfloat16), 'mp').astype(jnp.float32)  55.5 us
    psum x1, blocking collectives, shards(): lax.psum((part_first, part_second, gains_attn, gains_mlp), ('dp', 'mp'))  42.4 us
    all_gather x2, blocking collectives, backward_layer(): grad_whole = lax.all_gather(grad_low, 'mp', axis=1, tiled=True)  26.8 us
    all_gather x2, blocking collectives, forward_layer(): whole = lax.all_gather(slice_low, 'mp', axis=1, tiled=True)  20.8 us
  transfers between devices with their start and end apart: 11, of which 8 were waited for; matrix products, arithmetic and copies ran while one was open for 18% of the time, Pallas kernels for 0%

commit v1 on v0

v1 whole, which is shorter than its diff:
```python
import functools
import types

import jax
import jax.numpy as jnp
import numpy as np
from jax import lax
from jax.experimental import pallas as pl
from jax.experimental.pallas import tpu as pltpu
from jax.sharding import PartitionSpec as P

HEAD = 64
EPS = 1e-05
F32 = jnp.float32
BF16 = jnp.bfloat16
MESH = pl.DeviceIdType.MESH
GELU_A = 0.7978845608
GELU_B = 0.044715
HIDDEN_AXES = (((1,), (0,)), ((), ()))
SHARED_AXES = (((1,), (1,)), ((), ()))
TOKEN_AXES = (((0,), (0,)), ((), ()))

C_N1, C_OUT, C_N2, C_DN, C_GY, C_BP, C_GM, C_NP = 0, 2, 4, 6, 8, 10, 12, 14
C_CUR, C_COT, C_B1, C_MIX, C_GN, C_GC, C_SM, C_ALL = 16, 18, 20, 22, 24, 26, 28, 29
X_H0, X_AR, X_RS, X_GY, X_ARB, X_RSB, X_SM, X_ALL = 0, 2, 4, 6, 8, 10, 12, 13


def nn(a, b):
    return lax.dot_general(a, b, HIDDEN_AXES, preferred_element_type=F32)


def nt(a, b):
    return lax.dot_general(a, b, SHARED_AXES, preferred_element_type=F32)


def tn(a, b):
    return lax.dot_general(a, b, TOKEN_AXES, preferred_element_type=F32)


def center(values):
    shifted = values - jnp.mean(values, -1, keepdims=True)
    scale = lax.rsqrt(jnp.mean(shifted * shifted, -1, keepdims=True) + EPS)
    return shifted * scale, scale


def center_back(e, z, scale):
    return (e - jnp.mean(e, -1, keepdims=True) - z * jnp.mean(e * z, -1, keepdims=True)) * scale


def loop(count, step):
    def one(i, carry):
        step(i)
        return carry

    lax.fori_loop(0, count, one, 0)


def kernel(names, cfg, *refs):
    r = types.SimpleNamespace(**dict(zip(names, refs)))
    rows, width, heads, units, past, inner = cfg
    half, own_width = width // 2, width // 4
    chunk, sub = rows // 2, rows // 4
    block, strip = width // 8, own_width // 4
    count = 2

    m = lax.axis_index("mp")
    core, xx = lax.rem(m, 2), m // 2
    core_peer = {"mp": m + 1 - 2 * core}
    x_peer = {"mp": lax.rem(m + 2, 4)}
    if inner:
        d = lax.axis_index("dp")
        yy, zz = lax.rem(d, 2), d // 2
        y_peer = {"dp": d + 1 - 2 * yy}
        z_peers = [{"dp": lax.rem(d + 2 * step, 8)} for step in (1, 2, 3)]
    own_half = pl.ds(pl.multiple_of(xx * half, 128), half)
    far_half = pl.ds(pl.multiple_of((1 - xx) * half, 128), half)

    def at(k, who):
        return pl.ds(pl.multiple_of(k * chunk + who * sub, 32), sub)

    def of(k):
        return slice(k * chunk, (k + 1) * chunk)

    def mine(k):
        return at(k, core)

    def theirs(k):
        return at(k, 1 - core)

    def over_core(which, src, dst):
        return pltpu.make_async_remote_copy(
            src_ref=src,
            dst_ref=dst,
            send_sem=r.core_send.at[which],
            recv_sem=r.core_recv.at[which],
            device_id=core_peer,
            device_id_type=MESH,
        )

    def over_x(which, src, dst):
        return pltpu.make_async_remote_copy(
            src_ref=src,
            dst_ref=dst,
            send_sem=r.x_send.at[which],
            recv_sem=r.x_recv.at[which],
            device_id=x_peer,
            device_id_type=MESH,
        )

    loads = []
    for index, (src, dst) in enumerate(
        (
            (r.current, r.cur_t),
            (r.cotangent, r.cot_t),
            (r.cos_table, r.cosine),
            (r.sin_table, r.sine),
            (r.w_qkv, r.wq),
            (r.w_out, r.wo),
            (r.w_up, r.wu),
            (r.w_down, r.wd),
        )
    ):
        loads.append(pltpu.make_async_copy(src, dst, r.load_sem.at[index]))
        loads[index].start()

    def history_in(step, slot):
        return pltpu.make_async_copy(
            r.history.at[:, pl.ds(step * strip, strip), :], r.hist.at[slot], r.hist_in.at[slot]
        )

    history_in(0, 0).start()
    history_in(1, 1).start()

    barrier = pltpu.get_barrier_semaphore()
    peers = [core_peer, x_peer] + ([y_peer] + z_peers if inner else [])
    for peer in peers:
        pl.semaphore_signal(barrier, inc=1, device_id=peer, device_id_type=MESH)
    pl.semaphore_wait(barrier, len(peers))

    def c_n1(l, k):
        return over_core(C_N1 + k, r.n1.at[l, mine(k)], r.n1.at[l, mine(k)])

    def c_out(k):
        return over_core(C_OUT + k, r.cstage.at[k], r.crecv_fwd.at[k])

    def c_n2(l, k):
        return over_core(C_N2 + k, r.n2.at[l, mine(k)], r.n2.at[l, mine(k)])

    def c_dn(k):
        return over_core(C_DN + k, r.cstage.at[k], r.crecv_fwd.at[k])

    def c_gy(k):
        return over_core(C_GY + k, r.gy.at[mine(k)], r.gy.at[mine(k)])

    def c_bp(k):
        return over_core(C_BP + k, r.cstage.at[k], r.crecv_bwd.at[k])

    def c_gm(k):
        return over_core(C_GM + k, r.gm.at[mine(k)], r.gm.at[mine(k)])

    def c_np(k):
        return over_core(C_NP + k, r.cstage.at[k], r.crecv_bwd.at[k])

    def c_cur(k):
        return over_core(C_CUR + k, r.cur.at[theirs(k)], r.cv_cur.at[k])

    def c_cot(k):
        return over_core(C_COT + k, r.cot.at[theirs(k)], r.cv_cot.at[k])

    def c_b1(k):
        return over_core(C_B1 + k, r.blend1.at[theirs(k)], r.cv_b1.at[k])

    def c_mix(k):
        return over_core(C_MIX + k, r.cs_mix.at[k], r.cv_mix.at[k])

    def c_gn(k):
        return over_core(C_GN + k, r.cs_gn.at[k], r.cv_gn.at[k])

    def c_gc(k):
        return over_core(C_GC + k, r.cs_gc.at[k], r.cv_gc.at[k])

    def x_h0(l, k):
        return over_x(X_H0 + k, r.xs.at[l, k, :, own_half], r.xs.at[l, k, :, own_half])

    def x_ar(k):
        return over_x(X_AR + k, r.xstage.at[k], r.xrecv_whole.at[k])

    def x_rs(k):
        return over_x(X_RS + k, r.xstage_half.at[k], r.xrecv_half.at[k])

    def x_gy(k):
        return over_x(X_GY + k, r.gy.at[mine(k), own_half], r.gy.at[mine(k), own_half])

    def x_arb(k):
        return over_x(X_ARB + k, r.xstage.at[k], r.xrecv_whole.at[k])

    def x_rsb(k):
        return over_x(X_RSB + k, r.xstage_half.at[k], r.xrecv_half.at[k])

    def to_home(feature, recv, k):
        own, other = feature[mine(k), :].astype(F32), recv[k].astype(F32)
        first = core == 0
        r.home[:, :own_width] = jnp.where(first, own, other)
        r.home[:, own_width:] = jnp.where(first, other, own)
        return r.home[...]

    def from_home(values, keep, stage, k):
        first = core == 0
        low, high = values[:, :own_width], values[:, own_width:]
        keep[mine(k), :] = jnp.where(first, low, high).astype(keep.dtype)
        stage[k] = jnp.where(first, high, low).astype(stage.dtype)

    loads[0].wait()
    r.cur[...] = r.cur_t[...].astype(F32).T.astype(BF16)
    for k in range(count):
        c_cur(k).start()
    loads[1].wait()
    r.cot[...] = r.cot_t[...].astype(F32).T.astype(BF16)
    for k in range(count):
        c_cot(k).start()
    for k in range(count):
        c_cur(k).wait()
        r.xs[0, k, :, own_half] = to_home(r.cur, r.cv_cur, k).astype(BF16)
        x_h0(0, k).start()
    for k in (1, 0):
        c_cot(k).wait()
        home = to_home(r.cot, r.cv_cot, k)
        r.cot_home[k] = home.astype(BF16)
        r.gy[mine(k), own_half] = (r.second[past + 1] * home).astype(BF16)
        x_gy(k).start()

    loads[2].wait()
    loads[3].wait()
    segs = r.seq.shape[1]
    starts, ends = [], []
    total = jnp.int32(0)
    for index in range(segs):
        starts.append(total)
        total = total + r.seq[0, index]
        ends.append(total)
    cos_start = [r.cosine[pl.ds(jnp.clip(s, 0, rows - 1), 1), :] for s in starts]
    sin_start = [r.sine[pl.ds(jnp.clip(s, 0, rows - 1), 1), :] for s in starts]

    def make_tables(i):
        here = pl.ds(pl.multiple_of(i * sub, 32), sub)
        place = lax.broadcasted_iota(jnp.int32, (sub, 128), 0) + i * sub
        lane = lax.broadcasted_iota(jnp.int32, (sub, 128), 1)
        cos_s = jnp.broadcast_to(cos_start[0], (sub, 128))
        sin_s = jnp.broadcast_to(sin_start[0], (sub, 128))
        begin = jnp.zeros((sub, 1), jnp.int32)
        line = lax.broadcasted_iota(jnp.int32, (sub, 1), 0) + i * sub
        for index in range(1, segs):
            inside = place >= ends[index - 1]
            cos_s = jnp.where(inside, cos_start[index], cos_s)
            sin_s = jnp.where(inside, sin_start[index], sin_s)
            begin = jnp.where(line >= ends[index - 1], starts[index], begin)
        cos_t, sin_t = r.cosine[here, :], r.sine[here, :]
        sine = sin_t * cos_s - cos_t * sin_s
        r.rope_cos[here, :] = cos_t * cos_s + sin_t * sin_s
        r.rope_sin[here, :] = jnp.where(lax.rem(lane, HEAD) < HEAD // 2, -sine, sine)
        query = lax.broadcasted_iota(jnp.int32, (sub, rows), 0) + i * sub
        key = lax.broadcasted_iota(jnp.int32, (sub, rows), 1)
        r.bias[here, :] = jnp.where(
            (key <= query) & (key >= begin), 0.0, -1e30
        ).astype(BF16)

    loop(4, make_tables)

    def turn(values, here, sign):
        lane = lax.broadcasted_iota(jnp.int32, values.shape, 1)
        other = jnp.where(
            lax.rem(lane, HEAD) < HEAD // 2,
            pltpu.roll(values, 128 - HEAD // 2, 1),
            pltpu.roll(values, HEAD // 2, 1),
        )
        return values * r.rope_cos[here, :] + sign * (other * r.rope_sin[here, :])

    r.gains[...] = jnp.zeros_like(r.gains)
    r.dots[...] = jnp.zeros_like(r.dots)

    def fold(values):
        return jnp.sum(values, 0, keepdims=True)

    for step in range(4):
        slot = step % 2
        here = slice(step * strip, (step + 1) * strip)
        history_in(step, slot).wait()
        grad = r.cot_t[here, :].astype(F32)
        one = jnp.zeros((strip, rows), F32)
        two = jnp.zeros((strip, rows), F32)
        for j in range(past):
            value = r.hist[slot, j].astype(F32)
            one = one + r.first[j] * value
            two = two + r.second[j] * value
            r.dots[16 + j : 17 + j, :] += fold(value * grad)
        r.blend1_t[here, :] = one
        r.blend2_t[here, :] = two
        if step + 2 < 4:
            history_in(step + 2, slot).start()
    r.blend1[...] = r.blend1_t[...].T
    for k in range(count):
        c_b1(k).start()
    for k in range(count):
        c_b1(k).wait()
        r.blend1_home[k] = to_home(r.blend1, r.cv_b1, k)

    for load in loads[4:]:
        load.wait()

    def norm_in(l, k):
        x_h0(l, k).wait()
        z, scale = center(r.xs[l, k].astype(F32))
        r.z1[l, k] = z.astype(BF16)
        r.s1[l, k] = scale
        r.n1[l, mine(k)] = (z * r.gain_attn[pl.ds(l, 1), :]).astype(BF16)
        c_n1(l, k).start()

    def project(l, k):
        c_n1(l, k).wait()

        here = of(k)
        acc = nt(r.n1[l, here], r.wq[l])
        for h in range(heads):
            base = h * 3 * HEAD
            pair = turn(acc[:, base : base + 2 * HEAD], here, 1.0)
            r.q[l, h, here, :] = (pair[:, :HEAD] * HEAD**-0.5).astype(BF16)
            r.k[l, h, here, :] = pair[:, HEAD:].astype(BF16)
            r.v[l, h, here, :] = acc[:, base + 2 * HEAD : base + 3 * HEAD].astype(BF16)

    def attend(l, k):
        seen = (k + 1) * chunk
        here = of(k)
        for h in range(heads):
            scores = nt(r.q[l, h, here, :], r.k[l, h, :seen, :]) + r.bias[here, :seen].astype(F32)
            top = jnp.max(scores, -1, keepdims=True)
            probs = jnp.exp(scores - top)
            total = jnp.sum(probs, -1, keepdims=True)
            result = nn(probs.astype(BF16), r.v[l, h, :seen, :]) / total
            r.att[l, here, h * HEAD : (h + 1) * HEAD] = result.astype(BF16)
            r.lse[l, here, h : h + 1] = top + jnp.log(total)

    def split_sum(k, total, send):
        for who in (0, 1):

            @pl.when(core == who)
            def _(who=who):
                other = slice((1 - who) * sub, (2 - who) * sub)
                own = slice(who * sub, (who + 1) * sub)
                r.cstage[k] = total[other].astype(BF16)
                send.start()
                r.acc[k] = total[own]

    def project_out(l, k):
        split_sum(k, nn(r.att[l, of(k)], r.wo[l]), c_out(k))

    def chip_sum(k, arrival, received, onward):
        arrival.wait()
        total = r.acc[k] + received[k].astype(F32)
        r.acc[k] = total
        r.xstage[k] = total.astype(BF16)
        onward.start()

    def norm_mid(l, k):
        x_ar(k).wait()
        middle = r.xs[l, k].astype(F32) + r.acc[k] + r.xrecv_whole[k].astype(F32)
        r.mid[k] = middle
        z, scale = center(middle)
        r.z2[l, k] = z.astype(BF16)
        r.s2[l, k] = scale
        r.n2[l, mine(k)] = (z * r.gain_mlp[pl.ds(l, 1), :]).astype(BF16)
        c_n2(l, k).start()

    def feed(l, k):
        c_n2(l, k).wait()

        here = of(k)
        pre = nn(r.n2[l, here], r.wu[l])
        square = pre * pre
        wave = jnp.tanh(pre * (GELU_A + GELU_A * GELU_B * square))
        left = 0.5 + 0.5 * wave
        hidden = (pre * left).astype(BF16)
        slope = left + (0.5 - 0.5 * wave * wave) * pre * (
            GELU_A + 3.0 * GELU_A * GELU_B * square
        )
        r.hid[l, here] = hidden
        r.slope[l, here] = slope.astype(BF16)
        split_sum(k, nn(hidden, r.wd[l]), c_dn(k))

    def chip_scatter(k):
        c_dn(k).wait()
        far = r.acc[k, :, far_half] + r.crecv_fwd[k, :, far_half].astype(F32)
        r.xstage_half[k] = far.astype(BF16)
        x_rs(k).start()

    def block_out(l, k):
        x_rs(k).wait()
        y = (
            r.mid[k, :, own_half]
            + r.acc[k, :, own_half]
            + r.crecv_fwd[k, :, own_half].astype(F32)
            + r.xrecv_half[k].astype(F32)
        )
        grad = r.cot_home[k].astype(F32)

        @pl.when(l == 0)
        def _():
            r.y0[k] = y
            following = r.blend1_home[k] + r.first[past] * y
            r.xs[1, k, :, own_half] = following.astype(BF16)
            x_h0(1, k).start()
            r.dots[16 + past : 17 + past, :half] += fold(y * grad)

        @pl.when(l == 1)
        def _():
            rest = r.second[past] * r.y0[k] + r.second[past + 1] * y
            from_home(rest, r.blend1, r.cs_mix, k)
            c_mix(k).start()
            r.dots[17 + past : 18 + past, :half] += fold(y * grad)

    def forward(l):
        norm_in(l, 0)
        project(l, 0)

        @pl.when(l == 1)
        def _():
            block_out(0, 1)

        attend(l, 0)
        project_out(l, 0)
        norm_in(l, 1)
        chip_sum(0, c_out(0), r.crecv_fwd, x_ar(0))
        project(l, 1)
        attend(l, 1)
        project_out(l, 1)

        @pl.when(l == 0)
        def _():
            for k in (1, 0):
                x_gy(k).wait()
                c_gy(k).start()

        norm_mid(l, 0)
        chip_sum(1, c_out(1), r.crecv_fwd, x_ar(1))
        feed(l, 0)
        chip_scatter(0)
        norm_mid(l, 1)
        feed(l, 1)
        block_out(l, 0)
        chip_scatter(1)


    def feed_back(l, k):

        here = of(k)
        grad = nt(r.gy[here], r.wd[l])
        grad = (grad * r.slope[l, here].astype(F32)).astype(BF16)
        r.gp[here] = grad
        split_sum(k, nt(grad, r.wu[l]), c_bp(k))

    def mid_back(l, k):
        x_arb(k).wait()
        grad = r.acc[k] + r.xrecv_whole[k].astype(F32)
        z = r.z2[l, k].astype(F32)
        gain = r.gain_mlp[pl.ds(l, 1), :]
        once = jnp.where(xx == 0, 1.0, 0.0)
        r.gains[pl.ds(2 + l, 1), :] += once * fold(grad * z)
        total = r.gy[mine(k)].astype(F32) + center_back(grad * gain, z, r.s2[l, k])
        r.mid[k] = total
        r.gm[mine(k)] = total.astype(BF16)
        c_gm(k).start()

    def attend_back(l, k):
        c_gm(k).wait()
        seen = (k + 1) * chunk
        if k == 1:
            r.dqk[...] = jnp.zeros_like(r.dqk)
            r.dv[...] = jnp.zeros_like(r.dv)

        here = of(k)
        grads = nt(r.gm[here], r.wo[l]).astype(BF16)
        for h in range(heads):
            lanes = slice(h * HEAD, (h + 1) * HEAD)
            grad = grads[:, lanes]
            inner_sum = jnp.sum(
                grad.astype(F32) * r.att[l, here, lanes].astype(F32), -1, keepdims=True
            )
            q, keys, vals = r.q[l, h, here, :], r.k[l, h, :seen, :], r.v[l, h, :seen, :]
            scores = nt(q, keys) + r.bias[here, :seen].astype(F32)
            probs = jnp.exp(scores - r.lse[l, here, h : h + 1])
            grad_scores = (probs * (nt(grad, vals) - inner_sum)).astype(BF16)
            r.dqk[h, here, :HEAD] = nn(grad_scores, keys) * HEAD**-0.5
            r.dqk[h, :seen, HEAD:] += tn(grad_scores, q)
            r.dv[:seen, lanes] += tn(probs.astype(BF16), grad)
        for h in range(heads):
            base = h * 3 * HEAD
            pair = turn(r.dqk[h, here, :], here, -1.0)
            r.dqkv[here, base : base + 2 * HEAD] = pair.astype(BF16)
            r.dqkv[here, base + 2 * HEAD : base + 3 * HEAD] = r.dv[here, h * HEAD : (h + 1) * HEAD].astype(BF16)
        split_sum(k, nn(r.dqkv[here], r.wq[l]), c_np(k))

    def in_back(l, k):
        c_np(k).wait()
        grad = r.acc[k] + r.crecv_bwd[k].astype(F32)
        z = r.z1[l, k].astype(F32)
        gain = r.gain_attn[pl.ds(l, 1), :]
        r.gains[pl.ds(l, 1), :] += fold(grad * z)
        r.acc[k] = center_back(grad * gain, z, r.s1[l, k])
        r.xstage_half[k] = r.acc[k, :, far_half].astype(BF16)
        x_rsb(k).start()

    def block_back(l, k):
        x_rsb(k).wait()
        grad = r.mid[k, :, own_half] + r.acc[k, :, own_half] + r.xrecv_half[k].astype(F32)

        @pl.when(l == 1)
        def _():
            before = r.first[past] * grad + r.second[past] * r.cot_home[k].astype(F32)
            r.gy[mine(k), own_half] = before.astype(BF16)
            x_gy(k).start()
            from_home(grad, r.grad_next, r.cs_gn, k)
            c_gn(k).start()
            r.dots[past : past + 1, :half] += fold(r.y0[k] * grad)

        @pl.when(l == 0)
        def _():
            from_home(grad, r.grad_current, r.cs_gc, k)
            c_gc(k).start()

    def keep_grad(piece, columns, values):
        for j in range(8):
            r.grads[piece, j % 2, j // 2, :, columns] = values[j * block : (j + 1) * block].astype(BF16)

    def grads_down(l):
        first = 6 * (1 - l)
        values = tn(r.gy[...], r.hid[l])
        keep_grad(first, slice(None), values[:, :half])
        y_start(first)
        keep_grad(first + 1, slice(None), values[:, half:])
        y_start(first + 1)

    def grads_up(l):
        first = 6 * (1 - l) + 2
        values = tn(r.n2[l], r.gp[...])
        keep_grad(first, slice(None), values[:, :half])
        y_start(first)
        keep_grad(first + 1, slice(None), values[:, half:])
        y_start(first + 1)

    def grads_attend(l):
        first = 6 * (1 - l) + 4
        values = tn(r.n1[l], r.dqkv[...])
        keep_grad(first, slice(None), values[:, :half])
        y_start(first)
        keep_grad(first + 1, slice(0, own_width), values[:, half:])
        keep_grad(first + 1, slice(own_width, half), tn(r.gm[...], r.att[l]))
        y_start(first + 1)

    def y_copy(piece):
        return pltpu.make_async_remote_copy(
            src_ref=r.grads.at[piece, 1 - yy],
            dst_ref=r.y_in.at[piece],
            send_sem=r.y_send.at[piece],
            recv_sem=r.y_recv.at[piece],
            device_id=y_peer,
            device_id_type=MESH,
        )

    def z_copy(piece, step):
        return pltpu.make_async_remote_copy(
            src_ref=r.grads.at[piece, yy, lax.rem(zz + step, 4)],
            dst_ref=r.z_in.at[piece, step - 1],
            send_sem=r.z_send.at[piece, step - 1],
            recv_sem=r.z_recv.at[piece, step - 1],
            device_id=z_peers[step - 1],
            device_id_type=MESH,
        )

    def y_start(piece):
        if inner:
            y_copy(piece).start()

    def z_start(piece):
        if not inner:
            return
        y_copy(piece).wait()
        for z in range(4):
            both = r.grads[piece, yy, z].astype(F32) + r.y_in[piece, z].astype(F32)
            r.grads[piece, yy, z] = both.astype(BF16)
        for step in (2, 1, 3):
            z_copy(piece, step).start()

    def z_finish(piece):
        if not inner:
            return
        total = r.grads[piece, yy, zz].astype(F32)
        for step in (1, 2, 3):
            z_copy(piece, step).wait()
            total = total + r.z_in[piece, step - 1].astype(F32)
        r.parts[piece] = total

    loop(2, forward)
    for k in (1, 0):
        c_gy(k).wait()
    grads_down(1)
    block_out(1, 1)

    def backward(i):
        l = 1 - i

        @pl.when(l == 0)
        def _():
            x_gy(1).wait()
            c_gy(1).start()
            z_start(3)
            c_gy(1).wait()

        feed_back(l, 1)

        @pl.when(l == 0)
        def _():
            x_gy(0).wait()
            c_gy(0).start()

        chip_sum(1, c_bp(1), r.crecv_bwd, x_arb(1))

        @pl.when(l == 0)
        def _():
            c_gy(0).wait()

        feed_back(l, 0)

        @pl.when(l == 0)
        def _():
            grads_down(0)

        chip_sum(0, c_bp(0), r.crecv_bwd, x_arb(0))
        grads_up(l)

        @pl.when(l == 0)
        def _():
            z_start(4)

        mid_back(l, 1)

        @pl.when(l == 1)
        def _():
            z_start(0)

        attend_back(l, 1)
        mid_back(l, 0)

        @pl.when(l == 1)
        def _():
            z_start(1)

        @pl.when(l == 0)
        def _():
            z_start(5)

        in_back(l, 1)
        attend_back(l, 0)

        @pl.when(l == 1)
        def _():
            z_start(2)

        block_back(l, 1)

        @pl.when(l == 0)
        def _():
            z_start(6)

        in_back(l, 0)
        grads_attend(l)
        block_back(l, 0)

    loop(2, backward)

    for k in range(count):
        c_mix(k).wait()
        r.blend1[theirs(k), :] = r.cv_mix[k]
        c_gn(k).wait()
        r.grad_next[theirs(k), :] = r.cv_gn[k]
    r.mixed_t[...] = (r.blend2_t[...] + r.blend1[...].T).astype(BF16)
    r.grad_next_t[...] = r.grad_next[...].T

    z_start(7)
    for piece in range(5):
        z_finish(piece)

    history_in(0, 0).start()
    history_in(1, 1).start()
    for step in range(4):
        slot = step % 2
        here = slice(step * strip, (step + 1) * strip)
        history_in(step, slot).wait()
        grad_next = r.grad_next_t[here, :]
        for j in range(past):
            r.dots[j : j + 1, :] += fold(r.hist[slot, j].astype(F32) * grad_next)
        if step in (1, 3):
            z_start(8 + step // 2)
        if step + 2 < 4:
            history_in(step + 2, slot).start()

    z_finish(5)
    z_finish(6)

    small = r.small
    for i in range(width // 128):
        small[0, 4 * i : 4 * i + 4, :] = r.gains[:4, i * 128 : (i + 1) * 128]
    base = width // 32
    small[0, base : base + 32, :] = jnp.broadcast_to(
        jnp.sum(r.dots[...], -1, keepdims=True), (32, 128)
    )
    if inner:
        sm = over_core(C_SM, small.at[0], r.small_in.at[0])
        sm.start()
        sm.wait()
        small[1] = small[0] + r.small_in[0]
        sm = over_x(X_SM, small.at[1], r.small_in.at[1])
        sm.start()
        sm.wait()
        small[2] = small[1] + r.small_in[1]
        sm = pltpu.make_async_remote_copy(
            src_ref=small.at[2],
            dst_ref=r.small_in.at[2],
            send_sem=r.sm_send.at[0],
            recv_sem=r.sm_recv.at[0],
            device_id=y_peer,
            device_id_type=MESH,
        )
        sm.start()
        sm.wait()
        both = small[2] + r.small_in[2]
        small[3] = both
        sends = []
        for step in (1, 2, 3):
            sends.append(
                pltpu.make_async_remote_copy(
                    src_ref=small.at[3],
                    dst_ref=r.small_in.at[2 + step],
                    send_sem=r.sm_send.at[step],
                    recv_sem=r.sm_recv.at[step],
                    device_id=z_peers[step - 1],
                    device_id_type=MESH,
                )
            )
        for send in sends:
            send.start()
        for send in sends:
            send.wait()
        by_z = []
        for z in range(4):
            value = both
            for step in (1, 2, 3):
                value = jnp.where(lax.rem(z + step, 4) == zz, r.small_in[2 + step], value)
            by_z.append(value)
        r.sums[...] = (by_z[0] + by_z[1]) + (by_z[2] + by_z[3])
    else:
        r.sums[...] = small[0]

    for k in range(count):
        c_gc(k).wait()
        r.grad_current[theirs(k), :] = r.cv_gc[k].astype(F32)
    r.grad_current_t[...] = r.grad_current[...].T.astype(BF16)
    z_start(10)
    z_finish(7)
    z_finish(8)
    z_start(11)
    for piece in (9, 10, 11):
        z_finish(piece)
    if not inner:
        out = pltpu.make_async_copy(r.grads, r.raw, r.load_sem.at[0])
        out.start()
        out.wait()


def finish(names, past, *refs):
    r = types.SimpleNamespace(**dict(zip(names, refs)))
    grad, grad_next = r.cotangent[...].astype(F32), r.grad_next_t[...]
    for j in range(past):
        r.grad_history[j] = (r.first[j] * grad_next + r.second[j] * grad).astype(BF16)
    r.mixed[...] = r.mixed_t[...]
    r.grad_current[...] = r.grad_current_t[...]
    width = r.grad_gain_attn.shape[1]
    for i in range(width // 128):
        lanes = slice(i * 128, (i + 1) * 128)
        r.grad_gain_attn[:, lanes] = r.sums[4 * i : 4 * i + 2, :]
        r.grad_gain_mlp[:, lanes] = r.sums[4 * i + 2 : 4 * i + 4, :]
    base = width // 32
    dots = r.sums[base : base + 32, :]
    for j in range(past + 1):
        r.grad_first[j] = dots[j, 0]
    for j in range(past + 2):
        r.grad_second[j] = dots[16 + j, 0]
    half, own_width = width // 2, width // 4
    for l in (0, 1):
        first = 6 * (1 - l)
        for i in (0, 1):
            lanes = slice(i * half, (i + 1) * half)
            r.grad_down[l, :, lanes] = r.parts[first + i]
            r.grad_up[l, :, lanes] = r.parts[first + 2 + i]
        r.grad_qkv[l, :, :half] = r.parts[first + 4]
        r.grad_qkv[l, :, half:] = r.parts[first + 5, :, :own_width]
        r.grad_out[l] = r.parts[first + 5, :, own_width:].T


def tables(rows):
    freqs = 10000.0 ** (-2.0 * np.arange(HEAD // 2) / HEAD)
    angles = np.arange(rows)[:, None] * np.tile(freqs, 4)[None, :]
    return np.cos(angles).astype(np.float32), np.sin(angles).astype(np.float32)


def shards(
    n_dp,
    current,
    history,
    cotangent,
    seq_lengths,
    w_qkv,
    w_out,
    w_up,
    w_down,
    gain_attn,
    gain_mlp,
    dwa_first,
    dwa_second,
):
    rows, own_width = current.shape
    past = history.shape[0]
    layers, width, _ = w_qkv.shape
    heads = w_out.shape[1] // HEAD
    units = w_up.shape[2]
    sub, half, block = rows // 4, width // 2, width // 8
    inner = n_dp == 8
    cos_table, sin_table = tables(rows)

    hbm = pl.BlockSpec(memory_space=pl.ANY)
    vmem = pl.BlockSpec(memory_space=pltpu.VMEM)
    smem = pl.BlockSpec(memory_space=pltpu.SMEM)
    inputs = dict(
        current=(current.T, hbm),
        history=(history.transpose(0, 2, 1), hbm),
        cotangent=(cotangent.T, hbm),
        seq=(seq_lengths, smem),
        w_qkv=(w_qkv.transpose(0, 2, 1), hbm),
        w_out=(w_out, hbm),
        w_up=(w_up, hbm),
        w_down=(w_down, hbm),
        gain_attn=(gain_attn, vmem),
        gain_mlp=(gain_mlp, vmem),
        first=(dwa_first, smem),
        second=(dwa_second, smem),
        cos_table=(jnp.asarray(cos_table), hbm),
        sin_table=(jnp.asarray(sin_table), hbm),
    )

    def shape(dims, kind):
        return jax.ShapeDtypeStruct(dims, kind)

    small_rows = width // 32 + 32
    outputs = dict(
        mixed_t=(shape((own_width, rows), BF16), vmem),
        grad_current_t=(shape((own_width, rows), BF16), vmem),
        grad_next_t=(shape((own_width, rows), F32), vmem),
        sums=(shape((small_rows, 128), F32), vmem),
    )
    if inner:
        outputs.update(
            parts=(shape((6 * layers, block, half), F32), vmem),
        )
    else:
        outputs.update(
            raw=(shape((6 * layers, 2, 4, block, half), BF16), hbm),
        )

    def whole(kind=BF16, *lead):
        return pltpu.VMEM((*lead, rows, width), kind)

    def quarter(kind, *lead):
        return pltpu.VMEM((*lead, sub, width), kind)

    def quarter_half(kind, *lead):
        return pltpu.VMEM((*lead, sub, half), kind)

    def quarter_own(kind, *lead):
        return pltpu.VMEM((*lead, sub, own_width), kind)

    dma = pltpu.SemaphoreType.DMA
    scratch = dict(
        cur=pltpu.VMEM((rows, own_width), BF16),
        cot=pltpu.VMEM((rows, own_width), BF16),
        cosine=pltpu.VMEM((rows, 128), F32),
        sine=pltpu.VMEM((rows, 128), F32),
        rope_cos=pltpu.VMEM((rows, 128), F32),
        rope_sin=pltpu.VMEM((rows, 128), F32),
        bias=pltpu.VMEM((rows, rows), BF16),
        wq=pltpu.VMEM((layers, 3 * own_width, width), BF16),
        wo=pltpu.VMEM(w_out.shape, BF16),
        wu=pltpu.VMEM(w_up.shape, BF16),
        wd=pltpu.VMEM(w_down.shape, BF16),
        cur_t=pltpu.VMEM((own_width, rows), BF16),
        cot_t=pltpu.VMEM((own_width, rows), BF16),
        hist=pltpu.VMEM((2, past, own_width // 4, rows), BF16),
        blend1=pltpu.VMEM((rows, own_width), F32),
        blend1_t=pltpu.VMEM((own_width, rows), F32),
        blend2_t=pltpu.VMEM((own_width, rows), F32),
        grad_current=pltpu.VMEM((rows, own_width), F32),
        grad_next=pltpu.VMEM((rows, own_width), F32),
        blend1_home=quarter_half(F32, 2),
        home=quarter_half(F32),
        cot_home=quarter_half(BF16, 2),
        y0=quarter_half(F32, 2),
        xs=quarter(BF16, layers, 2),
        z1=quarter(BF16, layers, 2),
        z2=quarter(BF16, layers, 2),
        s1=pltpu.VMEM((layers, 2, sub, 1), F32),
        s2=pltpu.VMEM((layers, 2, sub, 1), F32),
        acc=quarter(F32, 2),
        mid=quarter(F32, 2),
        n1=whole(BF16, layers),
        n2=whole(BF16, layers),
        hid=pltpu.VMEM((layers, rows, units), BF16),
        slope=pltpu.VMEM((layers, rows, units), BF16),
        gp=pltpu.VMEM((rows, units), BF16),
        gy=whole(),
        gm=whole(),
        q=pltpu.VMEM((layers, heads, rows, HEAD), BF16),
        k=pltpu.VMEM((layers, heads, rows, HEAD), BF16),
        v=pltpu.VMEM((layers, heads, rows, HEAD), BF16),
        att=pltpu.VMEM((layers, rows, own_width), BF16),
        lse=pltpu.VMEM((layers, rows, heads), F32),
        dqk=pltpu.VMEM((heads, rows, 2 * HEAD), F32),
        dv=pltpu.VMEM((rows, own_width), F32),
        dqkv=pltpu.VMEM((rows, 3 * own_width), BF16),
        gains=pltpu.VMEM((8, width), F32),
        dots=pltpu.VMEM((32, rows), F32),
        small=pltpu.VMEM((4, small_rows, 128), F32),
        small_in=pltpu.VMEM((6, small_rows, 128), F32),
        cstage=quarter(BF16, 2),
        crecv_fwd=quarter(BF16, 2),
        crecv_bwd=quarter(BF16, 2),
        xstage=quarter(BF16, 2),
        xrecv_whole=quarter(BF16, 2),
        xstage_half=quarter_half(BF16, 2),
        xrecv_half=quarter_half(BF16, 2),
        cv_cur=quarter_own(BF16, 2),
        cv_cot=quarter_own(BF16, 2),
        cv_b1=quarter_own(F32, 2),
        cs_mix=quarter_own(F32, 2),
        cv_mix=quarter_own(F32, 2),
        cs_gn=quarter_own(F32, 2),
        cv_gn=quarter_own(F32, 2),
        cs_gc=quarter_own(BF16, 2),
        cv_gc=quarter_own(BF16, 2),
        grads=pltpu.VMEM((6 * layers, 2, 4, block, half), BF16),
        load_sem=dma((8,)),
        hist_in=dma((2,)),
        hist_out=dma((2,)),
        core_send=dma((C_ALL,)),
        core_recv=dma((C_ALL,)),
        x_send=dma((X_ALL,)),
        x_recv=dma((X_ALL,)),
    )
    if inner:
        scratch.update(
            y_in=pltpu.VMEM((6 * layers, 4, block, half), BF16),
            z_in=pltpu.VMEM((6 * layers, 3, block, half), BF16),
            y_send=dma((6 * layers,)),
            y_recv=dma((6 * layers,)),
            z_send=dma((6 * layers, 3)),
            z_recv=dma((6 * layers, 3)),
            sm_send=dma((4,)),
            sm_recv=dma((4,)),
        )
    names = [*inputs, *outputs, *scratch]
    results = pl.pallas_call(
        functools.partial(kernel, names, (rows, width, heads, units, past, inner)),
        out_shape=[o[0] for o in outputs.values()],
        in_specs=[i[1] for i in inputs.values()],
        out_specs=[o[1] for o in outputs.values()],
        scratch_shapes=[*scratch.values()],
        compiler_params=pltpu.CompilerParams(
            collective_id=0, has_side_effects=True, vmem_limit_bytes=63 * 2**20
        ),
    )(*[i[0] for i in inputs.values()])
    out = types.SimpleNamespace(**dict(zip(outputs, results)))
    if not inner:
        out.sums = lax.psum(out.sums, ("dp", "mp"))

        raw = out.raw.transpose(0, 2, 1, 3, 4).reshape(6 * layers, width, half).astype(F32)
        out.parts = lax.psum_scatter(raw, "dp", scatter_dimension=1, tiled=True)
    share = out.parts.shape[1]
    given = dict(
        cotangent=(cotangent.T, vmem),
        first=(dwa_first, smem),
        second=(dwa_second, smem),
        mixed_t=(out.mixed_t, vmem),
        grad_current_t=(out.grad_current_t, vmem),
        grad_next_t=(out.grad_next_t, vmem),
        sums=(out.sums, vmem),
        parts=(out.parts, vmem),
    )
    wanted = dict(
        mixed=(shape((own_width, rows), BF16), vmem),
        grad_current=(shape((own_width, rows), BF16), vmem),
        grad_history=(shape((past, own_width, rows), BF16), vmem),
        grad_qkv=(shape((layers, share, 3 * own_width), F32), vmem),
        grad_out=(shape((layers, own_width, share), F32), vmem),
        grad_up=(shape((layers, share, units), F32), vmem),
        grad_down=(shape((layers, share, units), F32), vmem),
        grad_gain_attn=(shape((layers, width), F32), vmem),
        grad_gain_mlp=(shape((layers, width), F32), vmem),
        grad_first=(shape((past + 1,), F32), smem),
        grad_second=(shape((past + 2,), F32), smem),
    )
    results = pl.pallas_call(
        functools.partial(finish, [*given, *wanted], past),
        out_shape=[o[0] for o in wanted.values()],
        in_specs=[i[1] for i in given.values()],
        out_specs=[o[1] for o in wanted.values()],
        compiler_params=pltpu.CompilerParams(vmem_limit_bytes=62 * 2**20),
    )(*[i[0] for i in given.values()])
    out = types.SimpleNamespace(**dict(zip(wanted, results)))
    return (
        out.mixed.T,
        out.grad_current.T,
        out.grad_history.transpose(0, 2, 1),
        out.grad_qkv,
        out.grad_out,
        out.grad_up,
        out.grad_down.transpose(0, 2, 1),
        out.grad_gain_attn,
        out.grad_gain_mlp,
        out.grad_first,
        out.grad_second,
    )


def solution(mesh):
    in_specs = (
        P("dp", "mp"),
        P(None, "dp", "mp"),
        P("dp", "mp"),
        P("dp", None),
        P(None, None, "mp"),
        P(None, "mp", None),
        P(None, None, "mp"),
        P(None, "mp", None),
        P(),
        P(),
        P(),
        P(),
    )
    out_specs = (
        P("dp", "mp"),
        P("dp", "mp"),
        P(None, "dp", "mp"),
        P(None, "dp", "mp"),
        P(None, "mp", "dp"),
        P(None, "dp", "mp"),
        P(None, "mp", "dp"),
        P(),
        P(),
        P(),
        P(),
    )
    return jax.shard_map(
        functools.partial(shards, mesh.shape["dp"]),
        mesh=mesh,
        in_specs=in_specs,
        out_specs=out_specs,
        check_vma=False,
    )
```

time: 858 us -> 178 us (0.21); the launches traced: 848 us -> 178 us
  waiting for transfers between devices: 482 us -> 0 us
  Pallas kernels: 0 us -> 177 us
  local copies, waits for them, and re-layouts: 115 us -> 0 us
  blocking collectives: 90.1 us -> 0 us
  other arithmetic: 75.3 us -> 0 us
  matrix products: 68.1 us -> 0 us
  between operations: 16.4 us -> 0.84 us
    unnamed x17 -> x0, waiting for transfers between devices: 268 us -> none
    pallas_call x0 -> x2, Pallas kernels: none -> 177 us  [the longest x1 171 us: shards(): pl.pallas_call(functools.partial(kernel, names, (rows, width, heads, unit...]
    psum x4 -> x0, waiting for transfers between devices: 119 us -> none  [the longest x2 63.1 us: backward_layer(): lax.psum(part_mid.astype(jnp.bfloat16), 'mp').astype(jnp.float32)]
    reduce_scatter x1 -> x0, waiting for transfers between devices: 95.1 us -> none  [shards(): lax.psum_scatter(together[2], 'dp', scatter_dimension=1, tiled=True)]
    dot_general x36 -> x0, matrix products: 68.1 us -> none  [the longest x2 8.81 us: one_block(): jnp.einsum('qhd,khd->hqk', grad_block, values, preferred_element_type=jnp...]
    unnamed x260 -> x0, local copies, waits for them, and re-layouts: 62.6 us -> none
    all_gather x4 -> x0, blocking collectives: 47.6 us -> none  [the longest x2 26.8 us: backward_layer(): grad_whole = lax.all_gather(grad_low, 'mp', axis=1, tiled=True)]
    psum x1 -> x0, blocking collectives: 42.4 us -> none  [shards(): lax.psum((part_first, part_second, gains_attn, gains_mlp), ('dp', 'mp'))]
  transfers between devices with their start and end apart: 11 -> 0, of which waited for: 8 -> 0; matrix products, arithmetic and copies ran while one was open for 18% -> 0% of each run, Pallas kernels for 0% -> 0%
where the time goes in v1:
time: 178 us
  Pallas kernels  177 us (99%)
    pallas_call x1, Pallas kernels, shards(): pl.pallas_call(functools.partial(kernel, names, (rows, width, heads, unit...  171 us
    pallas_call x1, Pallas kernels, shards(): pl.pallas_call(functools.partial(finish, [*given, *wanted], past), out_sh...  5.47 us

profile of v1, /device:TPU:0, one launch (start us, length us, event | category | flops | bytes accessed | tf_op | source)
XLA Modules:
  0.0 177.7 jit_solution(10372707226046748842)
XLA Ops:
  0.6 171.4 %shard_map.221 = (bf16[192,640]{1,0:T(8,128)(2,1)}, bf16[192,640]{1,0:T(8,128)(2,1)}, f32[192,640]{1,0:T(8,128)}, f32[56,128]{1,0:T(8,128)}, f32[12,96,384]{2,1,0:T(8,128)}) custom-call(bf16[192,640]{1,0:T(8,128)(2,1)} %bitcast.12, bf16[12,192,640]{2,1,0:T(8,128)(2,1)} %bitcast.8, bf16[192,640]{1,0:T(8,128)(2,1)} %bitcast.10, s32[1,4]{1,0:T(1,128)} %refs_3_.1, ...), custom_call_target="tpu_custom_call" | custom-call | tf_op jit(solution)/shard_map/pallas_call | solution.py:977
  172.1 5.5 %shard_map.222 = (bf16[192,640]{1,0:T(8,128)(2,1)}, bf16[192,640]{1,0:T(8,128)(2,1)}, bf16[12,192,640]{2,1,0:T(8,128)(2,1)}, f32[2,96,576]{2,1,0:T(8,128)}, f32[...) custom-call(bf16[192,640]{1,0:T(8,128)(2,1)} %bitcast.11, ...), custom_call_target="tpu_custom_call" | custom-call | tf_op jit(solution)/shard_map/pallas_call | solution.py:1017
